TPU v7x, 32 devices: a whole 2x2x4 slice. The times are simulated.
32 devices in a mesh: basin: 2 (over y), srow: 4 (over z), scol: 4 (over x, core).
Axes of the slice: x: 2, y: 2, z: 4, core: 2. Of those that a mesh axis runs over, the one named last changes fastest.
Arguments:
- top_inv: bfloat16 [4096, 2048], P(('basin', 'srow'), 'scol'), parts along dimension 0, may hold values from -0.125 to 0.125
- off_block: bfloat16 [16, 2048, 1024], P(('basin', 'scol'), 'srow'), parts along dimension 0, may hold values from -0.125 to 0.125
- kid_inv: bfloat16 [16, 1024, 1024], P(('basin', 'scol'), 'srow'), parts along dimension 0, may hold values from -0.1875 to 0.1875
- row_struct: int32 [16, 16], P(('basin', 'scol')), parts along dimension 0, may hold values 0 or 1
- labels: int32 [16, 1024], P(('basin', 'scol')), parts along dimension 0, may hold values from 0 to 31, never falling along the last dimension, each value on 1 to 64 neighbouring positions
Outputs:
- top_cov: float32 [4096, 2048], P(('basin', 'srow'), 'scol'), parts along dimension 0
- cross_cov: float32 [16, 2048, 1024], P(('basin', 'scol'), 'srow'), parts along dimension 0
- node_var: float32 [16, 1024], P(('basin', 'scol')), parts along dimension 0
- basin_var: float32 [64], P('basin'), parts along dimension 0
There are 2 independent parts, one for each index of `basin`. A program takes and returns all parts, laid end to end along the dimension named above; each array names one. Nothing has to cross between parts.
Inputs may be any that keep to these rules, and one draw needn't show every extreme that they name: `row_struct`: 1 where the supernode has nonzero entries in that block of 128 rows of the top separator, else 0. `labels`: along each supernode's 1024 nodes the label never falls; every label covers 1 to 64 consecutive nodes of every supernode, and some label covers exactly that many.
All inputs are finite; a program needn't handle non-finite values.
Results may differ from a plain program's by a relative error of at most 0.004.
Values may be sent and summed in bfloat16 or wider, within the bound.
A program may use at most 64 MiB of HBM per device.

v0:
```python
import jax
import jax.numpy as jnp
from jax import lax
from jax.sharding import PartitionSpec as P

RB = 128
G = 32


def per_device(top_inv, off_block, kid_inv, row_struct, labels):
    row_rank = lax.axis_index("srow")
    col_rank = lax.axis_index("scol")
    rows_top = top_inv.shape[0]
    cols_top = top_inv.shape[1]
    row_ids = row_rank * rows_top + jnp.arange(rows_top, dtype=jnp.int32)
    col_ids = col_rank * cols_top + jnp.arange(cols_top, dtype=jnp.int32)
    diagonal_one = (col_ids[None, :] == row_ids[:, None]).astype(top_inv.dtype)
    top_factor = jnp.where(col_ids[None, :] > row_ids[:, None], top_inv, diagonal_one)
    top_panel = lax.all_gather(top_factor, "srow", axis=0, tiled=True)
    block_sum = lax.psum_scatter(
        lax.dot_general(
            top_panel, top_factor, (((1,), (1,)), ((), ())), preferred_element_type=jnp.float32
        ),
        "scol",
        scatter_dimension=0,
        tiled=True,
    )
    top_cov = block_sum.T
    top_half = lax.all_gather(top_cov.astype(jnp.bfloat16), "scol", axis=1, tiled=True)
    kid_rows = kid_inv.shape[1]
    width = kid_inv.shape[2]
    kid_row_ids = row_rank * kid_rows + jnp.arange(kid_rows, dtype=jnp.int32)
    kid_col_ids = jnp.arange(width, dtype=jnp.int32)
    kid_one = (kid_row_ids[:, None] == kid_col_ids[None, :]).astype(kid_inv.dtype)
    kid_factor = jnp.where(kid_row_ids[:, None] > kid_col_ids[None, :], kid_inv, kid_one)
    local_rows = off_block.shape[1]
    block_ids = (row_rank * local_rows + jnp.arange(local_rows, dtype=jnp.int32)) // RB
    block_hits = (
        block_ids[:, None] == jnp.arange(row_struct.shape[1], dtype=jnp.int32)[None, :]
    ).astype(jnp.int32)
    kept_rows = jnp.sum(row_struct[:, None, :] * block_hits[None, :, :], axis=2)
    masked = jnp.where(kept_rows[:, :, None] != 0, off_block, jnp.zeros_like(off_block))
    product = jnp.einsum(
        "kac,kcw->kaw",
        masked,
        lax.all_gather(kid_factor, "srow", axis=1, tiled=True),
        preferred_element_type=jnp.float32,
    ).astype(jnp.bfloat16)
    image_sum = jnp.einsum(
        "am,kmw->kaw",
        top_half,
        lax.all_gather(product, "srow", axis=1, tiled=True),
        preferred_element_type=jnp.float32,
    )
    cross_cov = -image_sum
    own_part = jnp.sum(jnp.square(kid_factor.astype(jnp.float32)), axis=1) - jnp.sum(
        product.astype(jnp.float32) * cross_cov, axis=1
    )
    node_var = lax.psum(own_part, "srow")
    onehot = (labels[:, :, None] == jnp.arange(G, dtype=jnp.int32)[None, None, :]).astype(
        jnp.float32
    )
    local_counts = jnp.sum(onehot, axis=(0, 1))
    label_sum, counts = lax.psum((jnp.einsum("kw,kwg->g", node_var, onehot), local_counts), "scol")
    basin_var = label_sum / counts
    return (top_cov, cross_cov, node_var, basin_var)


def solution(mesh):
    placed = (
        P(("basin", "srow"), "scol"),
        P(("basin", "scol"), "srow", None),
        P(("basin", "scol"), "srow", None),
        P(("basin", "scol"), None),
        P(("basin", "scol"), None),
    )
    return jax.shard_map(
        per_device,
        mesh=mesh,
        in_specs=placed,
        out_specs=(
            P(("basin", "srow"), "scol"),
            P(("basin", "scol"), "srow", None),
            P(("basin", "scol"), None),
            P("basin"),
        ),
        check_vma=False,
    )
```

profile of v0, /device:TPU:0, one launch (start us, length us, event | category | flops | bytes accessed | tf_op | source)
XLA Modules:
  0.0 397.3 jit_solution(7836630926227850358)
XLA Ops:
  7.2 0.0 all-gather.5.cloned.1.call-start
  7.2 2.1 compare_select_fusion
  9.3 0.0 all-gather.5.cloned.1.call-update
  9.3 0.0 reduce-scatter.2.cloned.1.call-start
  9.4 49.4 %all-gather.5.cloned.1.call-done = bf16[2048,512]{1,0:T(8,128)(2,1)} async-done(((bf16[512,512]{1,0:T(8,128)(2,1)}), bf16[2048,512]{1,0:T(8,128)(2,1)}) %all-gather.5.cloned.1.call-update) | async-done | bytes 2097168 | tf_op jit(solution)/shard_map/all_gather | solution.py:19
  58.8 5.0 %fusion.16 = f32[2048,512]{1,0:T(8,128)} fusion(bf16[2048,512]{1,0:T(8,128)(2,1)} %all-gather.5.cloned.1.call-done, bf16[512,512]{1,0:T(8,128)(2,1)} %compare_select_fusion), kind=kOutput, calls=%fused_computation.37 | convolution fusion | flops 1073741824 | bytes 6815744 | tf_op jit(solution)/shard_map/dot_general | solution.py:21
  63.8 0.0 copy-start.2
  63.8 0.0 reduce-scatter.2.cloned.1.call-update
  63.8 0.0 all-gather.7.cloned.1.call-start
  63.9 0.3 iota_compare_fusion.1
  64.2 0.8 copy-done.2
  65.0 1.4 multiply_reduce_fusion.1
  66.4 0.0 copy-start.5
  66.4 0.0 copy-start.6
  66.4 0.0 all-gather.7.cloned.1.call-update
  66.5 0.0 all-gather.11.cloned.1.call-start
  66.5 40.7 %reduce-scatter.2.cloned.1.call-done = f32[512,512]{1,0:T(8,128)} async-done(((f32[2048,512]{1,0:T(8,128)}), f32[512,512]{1,0:T(8,128)}) %reduce-scatter.2.cloned.1.call-update) | async-done | bytes 1048592 | tf_op jit(solution)/shard_map/reduce_scatter | solution.py:20
  107.2 2.1 bitcast_convert_fusion
  109.2 0.0 all-gather.11.cloned.1.call-update
  109.3 0.0 all-gather.9.cloned.1.call-start
  109.4 0.0 copy-done.5
  109.4 0.1 multiply_reduce_fusion.2
  109.5 80.8 %all-gather.7.cloned.1.call-done = bf16[2,1024,1024]{2,1,0:T(8,128)(2,1)} async-done(((bf16[2,256,1024]{2,1,0:T(8,128)(2,1)}), bf16[2,1024,1024]{2,1,0:T(8,128)(2,1)}) %all-gather.7.cloned.1.call-update) | async-done | bytes 4194320 | tf_op jit(solution)/shard_map/all_gather | solution.py:46
  190.2 0.0 copy-done.6
  190.2 5.9 %fusion.4 = bf16[2,512,1024]{2,1,0:T(8,128)(2,1)} fusion(bf16[2,1024,1024]{2,1,0:T(8,128)(2,1)} %all-gather.7.cloned.1.call-done, bf16[2,512,1024]{2,1,0:T(8,128)(2,1)S(1)} %copy-done.6, pred[2,512]{1,0:T(4,128)(4,1)S(1)} %broadcast_compare_fusion), kind=kOutput, calls=%fused_computation.7 | convolution fusion | flops 2149580800 | bytes 8389632 | tf_op jit(solution)/shard_map/kac,kcw->kaw/dot_general | solution.py:43
  196.2 0.0 copy-start.3
  196.2 0.0 copy-start
  196.2 0.0 copy-start.1
  196.2 0.0 all-gather.9.cloned.1.call-update
  196.2 0.7 copy-done.3
  196.9 0.1 convert_reduce_fusion
  197.0 0.5 copy-done
  197.5 1.3 copy.12
  198.8 14.1 %all-gather.11.cloned.1.call-done = bf16[512,2048]{0,1:T(8,128)(2,1)} async-done(((bf16[512,512]{0,1:T(8,128)(2,1)}), bf16[512,2048]{0,1:T(8,128)(2,1)}) %all-gather.11.cloned.1.call-update) | async-done | bytes 2097168 | tf_op jit(solution)/shard_map/all_gather | solution.py:29
  212.9 151.7 %all-gather.9.cloned.1.call-done = bf16[2,2048,1024]{2,1,0:T(8,128)(2,1)} async-done(((bf16[2,512,1024]{2,1,0:T(8,128)(2,1)}), bf16[2,2048,1024]{2,1,0:T(8,128)(2,1)}) %all-gather.9.cloned.1.call-update) | async-done | bytes 8388624 | tf_op jit(solution)/shard_map/all_gather | solution.py:52
  364.6 0.0 copy-done.1
  364.6 11.0 %multiply_reduce_fusion = (f32[2,1024]{1,0:T(2,128)S(1)}, f32[2,512,1024]{2,1,0:T(8,128)}) fusion(bf16[2,512,1024]{2,1,0:T(8,128)(2,1)S(1)} %copy-done.1, bf16[2,2048,1024]{2,1,0:T(8,128)(2,1)} %all-gather.9.cloned.1.call-done, bf16[512,2048]{0,1:T(8,128)(2,1)} %all-gather.11.cloned.1.call-done), kind=kOutput, calls=%fused_computation | convolution fusion | flops 4299159552 | bytes 16785408 | tf_op jit(solution)/shard_map/am,kmw->kaw/dot_general | solution.py:49
  375.6 8.8 %psum.21 = f32[2,1024]{1,0:T(2,128)S(1)} all-reduce(f32[2,1024]{1,0:T(2,128)S(1)} %sub.10), channel_id=1, replica_groups=mesh['basin'=2,'srow'=4,'scol'=4] {'srow'}, use_global_device_ids=true, to_apply=%region_4.5 | all-reduce | flops 2048 | bytes 16384 | tf_op jit(solution)/shard_map/psum | solution.py:59
  384.4 0.0 copy-start.4
  384.5 0.2 convolution_bitcast_fusion
  384.6 5.6 %all-reduce = (f32[32]{0:T(128)S(1)}, f32[32]{0:T(128)S(1)}) all-reduce(f32[32]{0:T(128)S(1)} %convolution_bitcast_fusion, f32[32]{0:T(128)S(1)} %convert_reduce_fusion), channel_id=1, replica_groups=mesh['basin'=2,'srow'=4,'scol'=4] {'scol'}, use_global_device_ids=true, to_apply=%region_5.6 | all-reduce | flops 64 | bytes 512 | tf_op jit(solution)/shard_map/psum | solution.py:64
  390.3 0.5 div.19
  390.8 0.0 copy-done.4
  (6 shorter events, 0.0 us)
Async XLA Ops:
  7.2 51.6 %all-gather.5.cloned.1.call-start = ((), (), s32[]{:S(2)}) async-start(), calls=%async_computation.1 | async-start | bytes 2621440 | tf_op jit(solution)/shard_map/all_gather | solution.py:19
  9.3 97.8 %reduce-scatter.2.cloned.1.call-start = ((), (), s32[]{:S(2)}) async-start(), calls=%async_computation.2 | async-start | bytes 5242880 | tf_op jit(solution)/shard_map/reduce_scatter | solution.py:20
  63.8 1.2 copy-start.2
  63.8 126.4 %all-gather.7.cloned.1.call-start = ((), (), s32[]{:S(2)}) async-start(), calls=%async_computation.3 | async-start | bytes 5242880 | tf_op jit(solution)/shard_map/all_gather | solution.py:46
  66.4 42.9 %copy-start.5 = (s32[2,16]{1,0:T(2,128)S(1)}, s32[2,16]{1,0:T(2,128)}, u32[]{:S(2)}) copy-start(s32[2,16]{1,0:T(2,128)} %param.8) | copy-start | bytes 388
  66.4 123.8 %copy-start.6 = (bf16[2,512,1024]{2,1,0:T(8,128)(2,1)S(1)}, bf16[2,512,1024]{2,1,0:T(8,128)(2,1)}, u32[]{:S(2)}) copy-start(bf16[2,512,1024]{2,1,0:T(8,128)(2,1)} %param.6) | copy-start | bytes 6291460
  66.5 146.4 %all-gather.11.cloned.1.call-start = ((), (), s32[]{:S(2)}) async-start(), calls=%async_computation.5 | async-start | bytes 2621440 | tf_op jit(solution)/shard_map/all_gather | solution.py:29
  109.3 255.3 %all-gather.9.cloned.1.call-start = ((), (), s32[]{:S(2)}) async-start(), calls=%async_computation.4 | async-start | bytes 10485760 | tf_op jit(solution)/shard_map/all_gather | solution.py:52
  196.2 0.7 copy-start.3
  196.2 1.3 copy-start
  196.2 168.5 %copy-start.1 = (bf16[2,512,1024]{2,1,0:T(8,128)(2,1)S(1)}, bf16[2,512,1024]{2,1,0:T(8,128)(2,1)}, u32[]{:S(2)}) copy-start(bf16[2,512,1024]{2,1,0:T(8,128)(2,1)} %fusion.4) | copy-start | bytes 6291460
  384.4 6.3 %copy-start.4 = (f32[2,1024]{1,0:T(2,128)}, f32[2,1024]{1,0:T(2,128)S(1)}, u32[]{:S(2)}) copy-start(f32[2,1024]{1,0:T(2,128)S(1)} %psum.21) | copy-start | bytes 24580
Sparse Core Ops, SparseCore 0:
  10.1 48.6 all-gather.4
  63.9 43.2 reduce-scatter.1
  109.4 80.7 all-gather.6
  191.7 21.1 all-gather.10
  214.9 149.6 all-gather.8
where the time goes:
time: 398 us; the launch traced here: 397 us
  waiting for transfers between devices  337 us (85%)
  matrix products  22 us (6%)
  blocking collectives  14.4 us (4%)
  between operations  13.9 us (3%)
  other arithmetic  6.65 us (2%)
    all_gather x1, waiting for transfers between devices, per_device(): lax.all_gather(product, 'srow', axis=1, tiled=True)  152 us
    all_gather x1, waiting for transfers between devices, per_device(): lax.all_gather(kid_factor, 'srow', axis=1, tiled=True)  80.8 us
    all_gather x1, waiting for transfers between devices, per_device(): top_panel = lax.all_gather(top_factor, 'srow', axis=0, tiled=True)  49.4 us
    reduce_scatter x1, waiting for transfers between devices, per_device(): lax.psum_scatter(lax.dot_general(top_panel, top_factor, (((1,), (1,)), ((...  40.7 us
    all_gather x1, waiting for transfers between devices, per_device(): lax.all_gather(top_cov.astype(jnp.bfloat16), 'scol', axis=1, tiled=True)  14.1 us
    dot_general x1, matrix products, per_device(): jnp.einsum('am,kmw->kaw', top_half, lax.all_gather(product, 'srow', axis=...  11 us
    psum x1, blocking collectives, per_device(): node_var = lax.psum(own_part, 'srow')  8.81 us
  transfers between devices with their start and end apart: 5, of which 5 were waited for; matrix products, arithmetic and copies ran while one was open for 3% of the time, Pallas kernels for 0%

commit v1 on v0

--- a/solution.py
+++ b/solution.py
@@ -1,6 +1,8 @@
 import jax
 import jax.numpy as jnp
 from jax import lax
+from jax.experimental import pallas as pl
+from jax.experimental.pallas import tpu as pltpu
 from jax.sharding import PartitionSpec as P
 
 RB = 128
@@ -65,6 +67,240 @@
     basin_var = label_sum / counts
     return (top_cov, cross_cov, node_var, basin_var)
 
+MESH = pl.DeviceIdType.MESH
+
+
+def dot(a, b, b_dim):
+    return lax.dot_general(a, b, (((1,), (b_dim,)), ((), ())), preferred_element_type=jnp.float32)
+
+
+def fused(f_ref, off_ref, kid_ref, cov_ref, cross_ref, var_ref,
+          fall, offb, kidf, prod, th, acc, cbuf, vsum, vgot,
+          f_send, f_recv, off_send, off_recv, kid_send, kid_fwd, kid_recv,
+          p_send, p_recv, c_send, c_recv, v_send, v_recv):
+    b, z, d = lax.axis_index("basin"), lax.axis_index("srow"), lax.axis_index("scol")
+    h = lax.rem(d, 2)
+    base = d - h
+    sib = d + 1 - 2 * h
+    across = lax.rem(d + 2, 4)
+    far = lax.rem(sib + 2, 4)
+    tb = f_ref.shape[0]
+    kr = kid_ref.shape[1]
+    hw = kid_ref.shape[2] // 2
+    keeper = lax.div(z, 2)
+    slot = lax.rem(z, 2)
+    home = base + keeper
+    is_keeper = h == keeper
+    pending = []
+
+    barrier = pltpu.get_barrier_semaphore()
+    for s in range(1, 16):
+        other = lax.rem(z * 4 + d + s, 16)
+        pl.semaphore_signal(
+            barrier, inc=1, device_id=(b, lax.div(other, 4), lax.rem(other, 4)), device_id_type=MESH
+        )
+    pl.semaphore_wait(barrier, 15)
+
+    def send(cond, source, target, ssem, rsem, zz, cc):
+        copy = pltpu.make_async_remote_copy(
+            src_ref=source, dst_ref=target, send_sem=ssem, recv_sem=rsem,
+            device_id=(b, zz, cc), device_id_type=MESH,
+        )
+        pl.when(cond)(lambda: copy.start())
+        pending.append((cond, copy))
+
+    def local(cond, source, target, rsem):
+        pl.when(cond)(lambda: pltpu.make_async_copy(source, target, rsem).start())
+
+    def arrived(cond, target, rsem):
+        pl.when(cond)(lambda: pltpu.make_async_copy(target, target, rsem).wait())
+
+    def fan(s, r, source):
+        have = r <= d
+        target, rsem = fall.at[r, d], f_recv.at[r * 4 + d]
+        send(have & (r <= z) & (z < 3), source, target, f_send.at[s * 5], rsem, jnp.minimum(z + 1, 3), d)
+        send(have & (r >= z) & (z > 0), source, target, f_send.at[s * 5 + 1], rsem, jnp.maximum(z - 1, 0), d)
+        send(have, source, target, f_send.at[s * 5 + 2], rsem, z, across)
+        send(have, source, target, f_send.at[s * 5 + 3], rsem, z, sib)
+
+    order = (z, z + 1 - 2 * slot, jnp.where(z < 2, 2, 1), jnp.where(z < 2, 3, 0))
+    local(z <= d, f_ref, fall.at[z, d], f_recv.at[z * 4 + d])
+    fan(0, z, f_ref)
+
+    for part in (1, 0):
+        cols = pl.ds(part * hw, hw)
+        needed = (z >= 2) if part else (z >= 0)
+        for i in range(2):
+            kid = 2 * h + i
+            n = part * 2 + i
+            send(kid != z, off_ref.at[i, :, cols], offb.at[part, pl.ds(pl.multiple_of(slot * tb, tb), tb), :],
+                 off_send.at[n], off_recv.at[part * 2 + slot], kid, home)
+            local(kid == z, off_ref.at[i, :, cols], offb.at[part, pl.ds(pl.multiple_of(slot * tb, tb), tb), :],
+                  off_recv.at[part * 2 + slot])
+            send((kid != z) & needed, kid_ref.at[i, :, cols], kidf.at[part, z],
+                 kid_send.at[n], kid_recv.at[part * 4 + z], kid, d)
+            local((kid == z) & needed, kid_ref.at[i, :, cols], kidf.at[part, z], kid_recv.at[part * 4 + z])
+
+    def pass_on(s):
+        r = order[s]
+        arrived(r <= across, fall.at[r, across], f_recv.at[r * 4 + across])
+        send(r <= across, fall.at[r, across], fall.at[r, across], f_send.at[s * 5 + 4],
+             f_recv.at[r * 4 + across], z, sib)
+
+    for s in range(1, 4):
+        r = order[s]
+        arrived(r <= d, fall.at[r, d], f_recv.at[r * 4 + d])
+        fan(s, r, fall.at[r, d])
+        pass_on(s - 1)
+    pass_on(3)
+    arrived(z <= d, fall.at[z, d], f_recv.at[z * 4 + d])
+    for s in range(4):
+        for c in (sib, far):
+            arrived(order[s] <= c, fall.at[order[s], c], f_recv.at[order[s] * 4 + c])
+
+    def outer_block(r, c):
+        acc[...] = jnp.zeros_like(acc)
+
+        @pl.loop(jnp.maximum(r, c), 4)
+        def _(k):
+            acc[...] += dot(fall[r, k], fall[c, k], 1)
+
+    @pl.loop(0, 8)
+    def _(n):
+        i, j = lax.div(n, 4), lax.rem(n, 4)
+        outer_block(2 * h + i, j)
+        th[i, j] = acc[...].astype(jnp.bfloat16)
+
+    outer_block(z, d)
+    cov_ref[...] = acc[...]
+
+    half = pl.multiple_of(h * 2 * tb, 2 * tb)
+    for part in (1, 0):
+        cols = pl.ds(part * hw, hw)
+        low = 2 if part else 0
+        for zp in range(low, 4):
+            arrived(z >= 0, kidf.at[part, zp], kid_recv.at[part * 4 + zp])
+            send(is_keeper, kidf.at[part, zp], kidf.at[part, zp], kid_fwd.at[part * 4 + zp],
+                 kid_recv.at[part * 4 + zp], z, sib)
+        for q in range(2):
+            arrived(z >= 0, offb.at[part, pl.ds(q * tb, tb), :], off_recv.at[part * 2 + q])
+
+        @pl.loop(0, 2 * tb // 256)
+        def _(m):
+            rows = pl.ds(pl.multiple_of(m * 256, 256), 256)
+            lower = kidf[part, 2:4].reshape(2 * kr, hw)
+            total = dot(offb[1, rows, :], lower, 0)
+            if part == 0:
+                total += dot(offb[0, rows, :], kidf[0, 0:2].reshape(2 * kr, hw), 0)
+            prod[part, pl.ds(pl.multiple_of(half + m * 256, 256), 256), :] = total.astype(jnp.bfloat16)
+
+        mine = prod.at[part, pl.ds(half, 2 * tb), :]
+        send(z >= 0, mine, mine, p_send.at[part], p_recv.at[part], z, sib)
+
+        vsum[part] = jnp.zeros((8, hw), jnp.float32)
+
+        @pl.when(h == 0)
+        def _():
+            for zp in range(low, 4):
+                square = jnp.square(kidf[part, zp].astype(jnp.float32))
+                vsum[part] += jnp.sum(square.reshape(kr // 8, 8, hw), axis=0)
+
+        theirs = prod.at[part, pl.ds(pl.multiple_of((1 - h) * 2 * tb, 2 * tb), 2 * tb), :]
+        arrived(z >= 0, theirs, p_recv.at[part])
+        for i in range(2):
+            for m in range(2):
+                rows = pl.ds(m * (tb // 2), tb // 2)
+                total = dot(th[i, 0, rows, :], prod[part, 0:tb, :], 0)
+                for j in range(1, 4):
+                    total += dot(th[i, j, rows, :], prod[part, j * tb:(j + 1) * tb, :], 0)
+                own = prod[part, pl.ds(pl.multiple_of(half + i * tb + m * (tb // 2), tb // 2), tb // 2), :]
+                vsum[part] += jnp.sum((own.astype(jnp.float32) * total).reshape(tb // 16, 8, hw), axis=0)
+                cbuf[part, i, rows, :] = (-total).astype(jnp.bfloat16)
+            there = 2 * h + i
+            send(there != z, cbuf.at[part, i], cross_ref.at[slot, :, cols], c_send.at[part * 2 + i],
+                 c_recv.at[part * 2 + slot], there, home)
+            local(there == z, cbuf.at[part, i], cross_ref.at[slot, :, cols], c_recv.at[part * 2 + slot])
+        for there in range(4):
+            to_self = (there == z) & is_keeper
+            place = part * 4 + slot * 2 + h
+            send(jnp.logical_not(to_self), vsum.at[part], vgot.at[place], v_send.at[part * 4 + there],
+                 v_recv.at[place], there, home)
+            local(to_self, vsum.at[part], vgot.at[place], v_recv.at[place])
+
+    for part in (1, 0):
+        cols = pl.ds(part * hw, hw)
+        for q in range(2):
+            for hh in range(2):
+                arrived(z >= 0, vgot.at[part * 4 + q * 2 + hh], v_recv.at[part * 4 + q * 2 + hh])
+            both = vgot[part * 4 + q * 2] + vgot[part * 4 + q * 2 + 1]
+            var_ref[q:q + 1, cols] = jnp.sum(both, axis=0, keepdims=True)
+    for part in (1, 0):
+        for q in range(2):
+            place = cross_ref.at[q, :, pl.ds(part * hw, hw)]
+            arrived(z >= 0, place, c_recv.at[part * 2 + q])
+    for cond, copy in pending:
+        pl.when(cond)(copy.wait_send)
+
+
+def per_device_fused(top_inv, off_block, kid_inv, row_struct, labels):
+    row_rank = lax.axis_index("srow")
+    col_rank = lax.axis_index("scol")
+    tb = top_inv.shape[0]
+    row_ids = row_rank * tb + jnp.arange(tb, dtype=jnp.int32)
+    col_ids = col_rank * tb + jnp.arange(tb, dtype=jnp.int32)
+    diagonal_one = (col_ids[None, :] == row_ids[:, None]).astype(top_inv.dtype)
+    top_factor = jnp.where(col_ids[None, :] > row_ids[:, None], top_inv, diagonal_one)
+    kr = kid_inv.shape[1]
+    width = kid_inv.shape[2]
+    hw = width // 2
+    kid_row_ids = row_rank * kr + jnp.arange(kr, dtype=jnp.int32)
+    kid_col_ids = jnp.arange(width, dtype=jnp.int32)
+    kid_one = (kid_row_ids[:, None] == kid_col_ids[None, :]).astype(kid_inv.dtype)
+    kid_factor = jnp.where(kid_row_ids[:, None] > kid_col_ids[None, :], kid_inv, kid_one)
+    blocks = tb // RB
+    kept = lax.dynamic_slice_in_dim(row_struct, row_rank * blocks, blocks, axis=1)
+    kept_rows = jnp.repeat(kept, RB, axis=1)
+    masked = jnp.where(kept_rows[:, :, None] != 0, off_block, jnp.zeros_like(off_block))
+    bf = jnp.bfloat16
+    dma = pltpu.SemaphoreType.DMA
+    top_cov, cross_half, node_var = pl.pallas_call(
+        fused,
+        out_shape=(
+            jax.ShapeDtypeStruct((tb, tb), jnp.float32),
+            jax.ShapeDtypeStruct((2, tb, width), bf),
+            jax.ShapeDtypeStruct((2, width), jnp.float32),
+        ),
+        in_specs=[pl.BlockSpec(memory_space=pl.ANY)] * 3,
+        out_specs=(
+            pl.BlockSpec(memory_space=pltpu.VMEM),
+            pl.BlockSpec(memory_space=pl.ANY),
+            pl.BlockSpec(memory_space=pltpu.VMEM),
+        ),
+        scratch_shapes=[
+            pltpu.VMEM((4, 4, tb, tb), bf),
+            pltpu.VMEM((2, 2 * tb, hw), bf),
+            pltpu.VMEM((2, 4, kr, hw), bf),
+            pltpu.VMEM((2, 4 * tb, hw), bf),
+            pltpu.VMEM((2, 4, tb, tb), bf),
+            pltpu.VMEM((tb, tb), jnp.float32),
+            pltpu.VMEM((2, 2, tb, hw), bf),
+            pltpu.VMEM((2, 8, hw), jnp.float32),
+            pltpu.VMEM((8, 8, hw), jnp.float32),
+            dma((20,)), dma((16,)), dma((4,)), dma((4,)), dma((4,)), dma((8,)), dma((8,)),
+            dma((2,)), dma((2,)), dma((4,)), dma((4,)), dma((8,)), dma((8,)),
+        ],
+        compiler_params=pltpu.CompilerParams(
+            collective_id=0, has_side_effects=True, vmem_limit_bytes=48 * 1024 * 1024
+        ),
+    )(top_factor, masked, kid_factor)
+    cross_cov = cross_half.astype(jnp.float32)
+    onehot = (labels[:, :, None] == jnp.arange(G, dtype=jnp.int32)[None, None, :]).astype(
+        jnp.float32
+    )
+    local_counts = jnp.sum(onehot, axis=(0, 1))
+    label_sum, counts = lax.psum((jnp.einsum("kw,kwg->g", node_var, onehot), local_counts), "scol")
+    return (top_cov, cross_cov, node_var, label_sum / counts)
+
 
 def solution(mesh):
     placed = (
@@ -74,8 +310,9 @@
         P(("basin", "scol"), None),
         P(("basin", "scol"), None),
     )
+    small = mesh.shape["srow"] == 4 and mesh.shape["scol"] == 4
     return jax.shard_map(
-        per_device,
+        per_device_fused if small else per_device,
         mesh=mesh,
         in_specs=placed,
         out_specs=(

time: 398 us -> 177 us (0.44)
  waiting for transfers between devices: 337 us -> 0 us
  Pallas kernels: 0 us -> 129 us
  blocking collectives: 14.4 us -> 36.4 us
  matrix products: 22 us -> 0.16 us
  between operations: 13.9 us -> 0.7 us
    all_gather x4 -> x0, waiting for transfers between devices: 296 us -> none  [the longest x1 152 us: per_device(): lax.all_gather(product, 'srow', axis=1, tiled=True)]
    pallas_call x0 -> x1, Pallas kernels: none -> 129 us  [per_device_fused(): pl.pallas_call(fused, out_shape=(jax.ShapeDtypeStruct((tb, tb), jnp.float...]
    reduce_scatter x1 -> x0, waiting for transfers between devices: 40.7 us -> none  [per_device(): lax.psum_scatter(lax.dot_general(top_panel, top_factor, (((1,), (1,)), ((...]
    psum x2 -> x1, blocking collectives: 14.4 us -> 36.4 us  [per_device_fused(): lax.psum((jnp.einsum('kw,kwg->g', node_var, onehot), local_counts), 'scol')]
    dot_general x4 -> x1, matrix products: 22 us -> 0.16 us  [per_device_fused(): jnp.einsum('kw,kwg->g', node_var, onehot)]
  transfers between devices with their start and end apart: 5 -> 0, of which waited for: 5 -> 0; matrix products, arithmetic and copies ran while one was open for 3% -> 0% of each run, Pallas kernels for 0% -> 0%
where the time goes in v1:
time: 177 us
  Pallas kernels  129 us (73%)
  blocking collectives  36.4 us (21%)
  other arithmetic  8.89 us (5%)
    pallas_call x1, Pallas kernels, per_device_fused(): pl.pallas_call(fused, out_shape=(jax.ShapeDtypeStruct((tb, tb), jnp.float...  129 us
    psum x1, blocking collectives, per_device_fused(): lax.psum((jnp.einsum('kw,kwg->g', node_var, onehot), local_counts), 'scol')  36.4 us

profile of v1, /device:TPU:0, one launch (start us, length us, event | category | flops | bytes accessed | tf_op | source)
XLA Modules:
  0.0 177.1 jit_solution(4535772197674587274)
XLA Ops:
  0.6 1.3 compare_select_fusion.f_ref
  2.0 0.8 dynamic-slice_compare_fusion
  2.7 0.1 broadcast_bitcast_fusion
  2.8 0.0 copy-start
  2.8 3.2 %broadcast_select_fusion.off_ref = bf16[2,512,1024]{2,1,0:T(8,128)(2,1)} fusion(bf16[2,512,1024]{2,1,0:T(8,128)(2,1)} %param.6, pred[2,512]{1,0:T(4,128)(4,1)S(1)} %bitcast.9), kind=kLoop, calls=%fused_computation | loop fusion | flops 1048576 | bytes 4195328 | tf_op jit(solution)/shard_map/jit(_where)/select_n | solution.py:263
  6.0 0.3 fusion
  6.3 0.0 copy-done
  6.3 0.2 broadcast_select_fusion.1.kid_ref
  6.5 129.2 %shard_map.84 = (f32[512,512]{1,0:T(8,128)S(1)}, bf16[2,512,1024]{2,1,0:T(8,128)(2,1)S(1)}, f32[2,1024]{1,0:T(2,128)S(1)}) custom-call(bf16[512,512]{1,0:T(8,128)(2,1)S(1)} %compare_select_fusion.f_ref, bf16[2,512,1024]{2,1,0:T(8,128)(2,1)} %broadcast_select_fusion.off_ref, bf16[2,256,1024]{2,1,0:T(8,128)(2,1)S(1)} %broadcast_select_fusion.1.kid_ref), custom_call_target="tpu_custom_call" | custom-call | tf_op jit(solution)/shard_map/pallas_call | solution.py:266
  135.7 0.0 copy-start.1
  135.7 2.5 %convert_element_type.14 = f32[2,512,1024]{2,1,0:T(8,128)} convert(bf16[2,512,1024]{2,1,0:T(8,128)(2,1)S(1)} %get-tuple-element.8) | non-fusion elementwise | flops 1048576 | bytes 6291456 | tf_op jit(solution)/shard_map/convert_element_type | solution.py:296
  138.2 0.0 copy-done.1
  138.2 0.2 convolution_bitcast_fusion
  138.4 0.1 convert_reduce_fusion
  138.5 36.4 %all-reduce = (f32[32]{0:T(128)S(1)}, f32[32]{0:T(128)S(1)}) all-reduce(f32[32]{0:T(128)S(1)} %convolution_bitcast_fusion, f32[32]{0:T(128)S(1)} %convert_reduce_fusion), channel_id=1, replica_groups=mesh['basin'=2,'srow'=4,'scol'=4] {'scol'}, use_global_device_ids=true, to_apply=%region_0.1 | all-reduce | flops 64 | bytes 512 | tf_op jit(solution)/shard_map/psum | solution.py:301
  175.0 0.5 div.3
  175.5 1.0 copy.17
  176.5 0.6 copy.18
  (3 shorter events, 0.0 us)
Async XLA Ops:
  2.8 3.5 %copy-start = (bf16[2,256,1024]{2,1,0:T(8,128)(2,1)S(1)}, bf16[2,256,1024]{2,1,0:T(8,128)(2,1)}, u32[]{:S(2)}) copy-start(bf16[2,256,1024]{2,1,0:T(8,128)(2,1)} %param.7) | copy-start | bytes 3145732
  135.7 2.5 %copy-start.1 = (s32[2,1024]{1,0:T(2,128)S(1)}, s32[2,1024]{1,0:T(2,128)}, u32[]{:S(2)}) copy-start(s32[2,1024]{1,0:T(2,128)} %param.9) | copy-start | bytes 24580

commit v2 on v1

--- a/solution.py
+++ b/solution.py
@@ -74,10 +74,10 @@
     return lax.dot_general(a, b, (((1,), (b_dim,)), ((), ())), preferred_element_type=jnp.float32)
 
 
-def fused(f_ref, off_ref, kid_ref, cov_ref, cross_ref, var_ref,
-          fall, offb, kidf, prod, th, acc, cbuf, vsum, vgot,
+def fused(f_ref, off_ref, kid_ref, keep_ref, cov_ref, cross_ref, var_ref,
+          fall, offb, kidf, prod, th, acc, cbuf, vsum, vgot, kept,
           f_send, f_recv, off_send, off_recv, kid_send, kid_fwd, kid_recv,
-          p_send, p_recv, c_send, c_recv, v_send, v_recv):
+          p_send, p_recv, c_send, c_recv, v_send, v_recv, k_send, k_recv):
     b, z, d = lax.axis_index("basin"), lax.axis_index("srow"), lax.axis_index("scol")
     h = lax.rem(d, 2)
     base = d - h
@@ -127,19 +127,23 @@
     local(z <= d, f_ref, fall.at[z, d], f_recv.at[z * 4 + d])
     fan(0, z, f_ref)
 
-    for part in (1, 0):
+    def start_inputs(part):
         cols = pl.ds(part * hw, hw)
         needed = (z >= 2) if part else (z >= 0)
+        spot = pl.ds(pl.multiple_of(slot * tb, tb), tb)
         for i in range(2):
             kid = 2 * h + i
             n = part * 2 + i
-            send(kid != z, off_ref.at[i, :, cols], offb.at[part, pl.ds(pl.multiple_of(slot * tb, tb), tb), :],
-                 off_send.at[n], off_recv.at[part * 2 + slot], kid, home)
-            local(kid == z, off_ref.at[i, :, cols], offb.at[part, pl.ds(pl.multiple_of(slot * tb, tb), tb), :],
-                  off_recv.at[part * 2 + slot])
             send((kid != z) & needed, kid_ref.at[i, :, cols], kidf.at[part, z],
                  kid_send.at[n], kid_recv.at[part * 4 + z], kid, d)
             local((kid == z) & needed, kid_ref.at[i, :, cols], kidf.at[part, z], kid_recv.at[part * 4 + z])
+            send(kid != z, off_ref.at[i, :, cols], offb.at[part, spot, :],
+                 off_send.at[n], off_recv.at[part * 2 + slot], kid, home)
+            local(kid == z, off_ref.at[i, :, cols], offb.at[part, spot, :], off_recv.at[part * 2 + slot])
+
+    start_inputs(1)
+    send(is_keeper, keep_ref.at[slot], kept, k_send.at[0], k_recv.at[0], z, sib)
+    local(is_keeper, keep_ref.at[slot], kept, k_recv.at[0])
 
     def pass_on(s):
         r = order[s]
@@ -153,11 +157,8 @@
         fan(s, r, fall.at[r, d])
         pass_on(s - 1)
     pass_on(3)
-    arrived(z <= d, fall.at[z, d], f_recv.at[z * 4 + d])
-    for s in range(4):
-        for c in (sib, far):
-            arrived(order[s] <= c, fall.at[order[s], c], f_recv.at[order[s] * 4 + c])
-
+    start_inputs(0)
+    arrived(z >= 0, kept, k_recv.at[0])
     def outer_block(r, c):
         acc[...] = jnp.zeros_like(acc)
 
@@ -165,18 +166,8 @@
         def _(k):
             acc[...] += dot(fall[r, k], fall[c, k], 1)
 
-    @pl.loop(0, 8)
-    def _(n):
-        i, j = lax.div(n, 4), lax.rem(n, 4)
-        outer_block(2 * h + i, j)
-        th[i, j] = acc[...].astype(jnp.bfloat16)
-
-    outer_block(z, d)
-    cov_ref[...] = acc[...]
-
     half = pl.multiple_of(h * 2 * tb, 2 * tb)
-    for part in (1, 0):
-        cols = pl.ds(part * hw, hw)
+    def make_product(part):
         low = 2 if part else 0
         for zp in range(low, 4):
             arrived(z >= 0, kidf.at[part, zp], kid_recv.at[part * 4 + zp])
@@ -192,7 +183,9 @@
             total = dot(offb[1, rows, :], lower, 0)
             if part == 0:
                 total += dot(offb[0, rows, :], kidf[0, 0:2].reshape(2 * kr, hw), 0)
-            prod[part, pl.ds(pl.multiple_of(half + m * 256, 256), 256), :] = total.astype(jnp.bfloat16)
+            for t in range(2):
+                cut = total[t * RB:(t + 1) * RB] * kept[h * 8 + m * 2 + t][0:1]
+                prod[part, pl.ds(pl.multiple_of(half + m * 256 + t * RB, RB), RB), :] = cut.astype(jnp.bfloat16)
 
         mine = prod.at[part, pl.ds(half, 2 * tb), :]
         send(z >= 0, mine, mine, p_send.at[part], p_recv.at[part], z, sib)
@@ -205,6 +198,8 @@
                 square = jnp.square(kidf[part, zp].astype(jnp.float32))
                 vsum[part] += jnp.sum(square.reshape(kr // 8, 8, hw), axis=0)
 
+    def make_cross(part):
+        cols = pl.ds(part * hw, hw)
         theirs = prod.at[part, pl.ds(pl.multiple_of((1 - h) * 2 * tb, 2 * tb), 2 * tb), :]
         arrived(z >= 0, theirs, p_recv.at[part])
         for i in range(2):
@@ -227,6 +222,24 @@
                  v_recv.at[place], there, home)
             local(to_self, vsum.at[part], vgot.at[place], v_recv.at[place])
 
+    make_product(1)
+    arrived(z <= d, fall.at[z, d], f_recv.at[z * 4 + d])
+    for s in range(4):
+        for c in (sib, far):
+            arrived(order[s] <= c, fall.at[order[s], c], f_recv.at[order[s] * 4 + c])
+
+    @pl.loop(0, 8)
+    def _(n):
+        i, j = lax.div(n, 4), lax.rem(n, 4)
+        outer_block(2 * h + i, j)
+        th[i, j] = acc[...].astype(jnp.bfloat16)
+
+    make_cross(1)
+    make_product(0)
+    make_cross(0)
+    outer_block(z, d)
+    cov_ref[...] = acc[...]
+
     for part in (1, 0):
         cols = pl.ds(part * hw, hw)
         for q in range(2):
@@ -257,10 +270,9 @@
     kid_col_ids = jnp.arange(width, dtype=jnp.int32)
     kid_one = (kid_row_ids[:, None] == kid_col_ids[None, :]).astype(kid_inv.dtype)
     kid_factor = jnp.where(kid_row_ids[:, None] > kid_col_ids[None, :], kid_inv, kid_one)
-    blocks = tb // RB
-    kept = lax.dynamic_slice_in_dim(row_struct, row_rank * blocks, blocks, axis=1)
-    kept_rows = jnp.repeat(kept, RB, axis=1)
-    masked = jnp.where(kept_rows[:, :, None] != 0, off_block, jnp.zeros_like(off_block))
+    keep = jnp.broadcast_to(
+        (row_struct != 0).astype(jnp.float32)[:, :, None, None], row_struct.shape + (8, hw)
+    )
     bf = jnp.bfloat16
     dma = pltpu.SemaphoreType.DMA
     top_cov, cross_half, node_var = pl.pallas_call(
@@ -270,7 +282,7 @@
             jax.ShapeDtypeStruct((2, tb, width), bf),
             jax.ShapeDtypeStruct((2, width), jnp.float32),
         ),
-        in_specs=[pl.BlockSpec(memory_space=pl.ANY)] * 3,
+        in_specs=[pl.BlockSpec(memory_space=pl.ANY)] * 4,
         out_specs=(
             pl.BlockSpec(memory_space=pltpu.VMEM),
             pl.BlockSpec(memory_space=pl.ANY),
@@ -286,13 +298,15 @@
             pltpu.VMEM((2, 2, tb, hw), bf),
             pltpu.VMEM((2, 8, hw), jnp.float32),
             pltpu.VMEM((8, 8, hw), jnp.float32),
+            pltpu.VMEM((row_struct.shape[1], 8, hw), jnp.float32),
             dma((20,)), dma((16,)), dma((4,)), dma((4,)), dma((4,)), dma((8,)), dma((8,)),
             dma((2,)), dma((2,)), dma((4,)), dma((4,)), dma((8,)), dma((8,)),
+            dma((1,)), dma((1,)),
         ],
         compiler_params=pltpu.CompilerParams(
             collective_id=0, has_side_effects=True, vmem_limit_bytes=48 * 1024 * 1024
         ),
-    )(top_factor, masked, kid_factor)
+    )(top_factor, off_block, kid_factor, keep)
     cross_cov = cross_half.astype(jnp.float32)
     onehot = (labels[:, :, None] == jnp.arange(G, dtype=jnp.int32)[None, None, :]).astype(
         jnp.float32

time: 177 us -> 154 us (0.87)
  blocking collectives: 36.4 us -> 22.5 us
  Pallas kernels: 129 us -> 124 us
  other arithmetic: 8.89 us -> 5 us
    psum x1, blocking collectives: 36.4 us -> 22.5 us  [per_device_fused(): lax.psum((jnp.einsum('kw,kwg->g', node_var, onehot), local_counts), 'scol')]
    pallas_call x1, Pallas kernels: 129 us -> 124 us  [per_device_fused(): pl.pallas_call(fused, out_shape=(jax.ShapeDtypeStruct((tb, tb), jnp.float...]
    select_n x1 -> x0, other arithmetic: 3.22 us -> none  [per_device_fused(): jnp.where(kept_rows[:, :, None] != 0, off_block, jnp.zeros_like(off_block))]
where the time goes in v2:
time: 154 us
  Pallas kernels  124 us (81%)
  blocking collectives  22.5 us (15%)
  other arithmetic  5 us (3%)
  local copies, waits for them, and re-layouts  1.85 us (1%)
    pallas_call x1, Pallas kernels, per_device_fused(): pl.pallas_call(fused, out_shape=(jax.ShapeDtypeStruct((tb, tb), jnp.float...  124 us
    psum x1, blocking collectives, per_device_fused(): lax.psum((jnp.einsum('kw,kwg->g', node_var, onehot), local_counts), 'scol')  22.5 us

profile of v2, /device:TPU:0, one launch (start us, length us, event | category | flops | bytes accessed | tf_op | source)
XLA Modules:
  0.0 154.1 jit_solution(2723067608960792516)
XLA Ops:
  0.6 0.0 copy-start
  0.7 1.4 compare_select_fusion.f_ref
  2.0 0.0 copy-start.2
  2.1 0.3 fusion
  2.4 0.0 copy-done
  2.4 0.2 broadcast_select_fusion.kid_ref
  2.6 0.2 copy-done.2
  2.7 0.1 broadcast_in_dim.12.keep_ref
  2.8 123.9 %shard_map.84 = (f32[512,512]{1,0:T(8,128)S(1)}, bf16[2,512,1024]{2,1,0:T(8,128)(2,1)S(1)}, f32[2,1024]{1,0:T(2,128)S(1)}) custom-call(bf16[512,512]{1,0:T(8,128)(2,1)S(1)} %compare_select_fusion.f_ref, bf16[2,512,1024]{2,1,0:T(8,128)(2,1)} %off_ref.1, bf16[2,256,1024]{2,1,0:T(8,128)(2,1)S(1)} %broadcast_select_fusion.kid_ref, ...), custom_call_target="tpu_custom_call" | custom-call | tf_op jit(solution)/shard_map/pallas_call | solution.py:278
  126.7 0.0 copy-start.1
  126.8 2.5 %convert_element_type.18 = f32[2,512,1024]{2,1,0:T(8,128)} convert(bf16[2,512,1024]{2,1,0:T(8,128)(2,1)S(1)} %get-tuple-element.8) | non-fusion elementwise | flops 1048576 | bytes 6291456 | tf_op jit(solution)/shard_map/convert_element_type | solution.py:310
  129.2 0.0 copy-done.1
  129.2 0.2 convolution_bitcast_fusion
  129.4 0.1 convert_reduce_fusion
  129.5 22.5 %all-reduce = (f32[32]{0:T(128)S(1)}, f32[32]{0:T(128)S(1)}) all-reduce(f32[32]{0:T(128)S(1)} %convolution_bitcast_fusion, f32[32]{0:T(128)S(1)} %convert_reduce_fusion), channel_id=1, replica_groups=mesh['basin'=2,'srow'=4,'scol'=4] {'scol'}, use_global_device_ids=true, to_apply=%region_0.1 | all-reduce | flops 64 | bytes 512 | tf_op jit(solution)/shard_map/psum | solution.py:315
  152.0 0.5 div.3
  152.5 1.0 copy.14
  153.5 0.6 copy.15
  (3 shorter events, 0.0 us)
Async XLA Ops:
  0.6 1.7 %copy-start = (bf16[2,256,1024]{2,1,0:T(8,128)(2,1)S(1)}, bf16[2,256,1024]{2,1,0:T(8,128)(2,1)}, u32[]{:S(2)}) copy-start(bf16[2,256,1024]{2,1,0:T(8,128)(2,1)} %param.7) | copy-start | bytes 3145732
  2.0 0.7 copy-start.2
  126.7 2.5 %copy-start.1 = (s32[2,1024]{1,0:T(2,128)S(1)}, s32[2,1024]{1,0:T(2,128)}, u32[]{:S(2)}) copy-start(s32[2,1024]{1,0:T(2,128)} %param.9) | copy-start | bytes 24580

commit v3 on v2

--- a/solution.py
+++ b/solution.py
@@ -74,10 +74,10 @@
     return lax.dot_general(a, b, (((1,), (b_dim,)), ((), ())), preferred_element_type=jnp.float32)
 
 
-def fused(f_ref, off_ref, kid_ref, keep_ref, cov_ref, cross_ref, var_ref,
-          fall, offb, kidf, prod, th, acc, cbuf, vsum, vgot, kept,
+def fused(f_ref, off_ref, kid_ref, keep_ref, lab_ref, cov_ref, cross_ref, var_ref, mean_ref,
+          fall, offb, kidf, prod, th, acc, cbuf, vsum, vgot, kept, tally,
           f_send, f_recv, off_send, off_recv, kid_send, kid_fwd, kid_recv,
-          p_send, p_recv, c_send, c_recv, v_send, v_recv, k_send, k_recv):
+          p_send, p_recv, c_send, c_recv, v_send, v_recv, k_send, k_recv, t_send, t_recv):
     b, z, d = lax.axis_index("basin"), lax.axis_index("srow"), lax.axis_index("scol")
     h = lax.rem(d, 2)
     base = d - h
@@ -93,6 +93,12 @@
     is_keeper = h == keeper
     pending = []
 
+    def kid_view(part, zp):
+        return kidf.at[part, zp, :, pl.ds(0, hw // 2 if zp == 2 * part else hw)]
+
+    for part in (0, 1):
+        kidf[part, 2 * part, :, hw // 2:] = jnp.zeros((kr, hw - hw // 2), kidf.dtype)
+
     barrier = pltpu.get_barrier_semaphore()
     for s in range(1, 16):
         other = lax.rem(z * 4 + d + s, 16)
@@ -115,13 +121,19 @@
     def arrived(cond, target, rsem):
         pl.when(cond)(lambda: pltpu.make_async_copy(target, target, rsem).wait())
 
+    def columns(r):
+        moved = (r == 3) & (z < 3)
+        return jnp.where(moved, across, d), jnp.where(moved, d, across)
+
     def fan(s, r, source):
-        have = r <= d
-        target, rsem = fall.at[r, d], f_recv.at[r * 4 + d]
-        send(have & (r <= z) & (z < 3), source, target, f_send.at[s * 5], rsem, jnp.minimum(z + 1, 3), d)
-        send(have & (r >= z) & (z > 0), source, target, f_send.at[s * 5 + 1], rsem, jnp.maximum(z - 1, 0), d)
-        send(have, source, target, f_send.at[s * 5 + 2], rsem, z, across)
-        send(have, source, target, f_send.at[s * 5 + 3], rsem, z, sib)
+        c, _ = columns(r)
+        have = r <= c
+        target, rsem = fall.at[r, c], f_recv.at[r * 4 + c]
+        send(have & (r <= z) & (z < 3), source, target, f_send.at[s * 6], rsem, jnp.minimum(z + 1, 3), d)
+        send(have & (r >= z) & (z > 0) & (z < 3), source, target, f_send.at[s * 6 + 1], rsem,
+             jnp.maximum(z - 1, 0), d)
+        send(have, source, target, f_send.at[s * 6 + 2], rsem, z, across)
+        send(have, source, target, f_send.at[s * 6 + 3], rsem, z, sib)
 
     order = (z, z + 1 - 2 * slot, jnp.where(z < 2, 2, 1), jnp.where(z < 2, 3, 0))
     local(z <= d, f_ref, fall.at[z, d], f_recv.at[z * 4 + d])
@@ -134,9 +146,13 @@
         for i in range(2):
             kid = 2 * h + i
             n = part * 2 + i
-            send((kid != z) & needed, kid_ref.at[i, :, cols], kidf.at[part, z],
-                 kid_send.at[n], kid_recv.at[part * 4 + z], kid, d)
-            local((kid == z) & needed, kid_ref.at[i, :, cols], kidf.at[part, z], kid_recv.at[part * 4 + z])
+            for narrow in (True, False):
+                width = hw // 2 if narrow else hw
+                chosen = needed & ((z == 2 * part) if narrow else (z != 2 * part))
+                source = kid_ref.at[i, :, pl.ds(part * hw, width)]
+                target = kidf.at[part, z, :, pl.ds(0, width)]
+                send((kid != z) & chosen, source, target, kid_send.at[n], kid_recv.at[part * 4 + z], kid, d)
+                local((kid == z) & chosen, source, target, kid_recv.at[part * 4 + z])
             send(kid != z, off_ref.at[i, :, cols], offb.at[part, spot, :],
                  off_send.at[n], off_recv.at[part * 2 + slot], kid, home)
             local(kid == z, off_ref.at[i, :, cols], offb.at[part, spot, :], off_recv.at[part * 2 + slot])
@@ -147,15 +163,19 @@
 
     def pass_on(s):
         r = order[s]
-        arrived(r <= across, fall.at[r, across], f_recv.at[r * 4 + across])
-        send(r <= across, fall.at[r, across], fall.at[r, across], f_send.at[s * 5 + 4],
-             f_recv.at[r * 4 + across], z, sib)
+        _, c = columns(r)
+        target, rsem = fall.at[r, c], f_recv.at[r * 4 + c]
+        arrived(r <= c, target, rsem)
+        send(r <= c, target, target, f_send.at[s * 6 + 4], rsem, z, sib)
+        send((r <= c) & (r == 3) & (z == 3), target, target, f_send.at[s * 6 + 5], rsem,
+             jnp.maximum(z - 1, 0), d)
 
     for s in range(1, 4):
+        pass_on(s - 1)
         r = order[s]
-        arrived(r <= d, fall.at[r, d], f_recv.at[r * 4 + d])
-        fan(s, r, fall.at[r, d])
-        pass_on(s - 1)
+        c, _ = columns(r)
+        arrived(r <= c, fall.at[r, c], f_recv.at[r * 4 + c])
+        fan(s, r, fall.at[r, c])
     pass_on(3)
     start_inputs(0)
     arrived(z >= 0, kept, k_recv.at[0])
@@ -170,8 +190,9 @@
     def make_product(part):
         low = 2 if part else 0
         for zp in range(low, 4):
-            arrived(z >= 0, kidf.at[part, zp], kid_recv.at[part * 4 + zp])
-            send(is_keeper, kidf.at[part, zp], kidf.at[part, zp], kid_fwd.at[part * 4 + zp],
+            view = kid_view(part, zp)
+            arrived(z >= 0, view, kid_recv.at[part * 4 + zp])
+            send(is_keeper, view, view, kid_fwd.at[part * 4 + zp],
                  kid_recv.at[part * 4 + zp], z, sib)
         for q in range(2):
             arrived(z >= 0, offb.at[part, pl.ds(q * tb, tb), :], off_recv.at[part * 2 + q])
@@ -247,6 +268,26 @@
                 arrived(z >= 0, vgot.at[part * 4 + q * 2 + hh], v_recv.at[part * 4 + q * 2 + hh])
             both = vgot[part * 4 + q * 2] + vgot[part * 4 + q * 2 + 1]
             var_ref[q:q + 1, cols] = jnp.sum(both, axis=0, keepdims=True)
+    groups = lax.broadcasted_iota(jnp.int32, (G, 2 * hw), 0)
+    sums = jnp.zeros((G, 128), jnp.float32)
+    counts = jnp.zeros((G, 128), jnp.float32)
+    for q in range(2):
+        hit = groups == lab_ref[q:q + 1, :]
+        terms = jnp.where(hit, var_ref[q:q + 1, :], 0.0)
+        ones = jnp.where(hit, 1.0, 0.0)
+        for t in range(2 * hw // 128):
+            sums += terms[:, t * 128:(t + 1) * 128]
+            counts += ones[:, t * 128:(t + 1) * 128]
+    tally[d, 0] = sums
+    tally[d, 1] = counts
+    for n, c in enumerate((sib, across, far)):
+        send(z >= 0, tally.at[d], tally.at[d], t_send.at[n], t_recv.at[d], z, c)
+    for c in (sib, across, far):
+        arrived(z >= 0, tally.at[c], t_recv.at[c])
+    sums = tally[0, 0] + tally[1, 0] + tally[2, 0] + tally[3, 0]
+    counts = tally[0, 1] + tally[1, 1] + tally[2, 1] + tally[3, 1]
+    mean = jnp.sum(sums, axis=1, keepdims=True) / jnp.sum(counts, axis=1, keepdims=True)
+    mean_ref[...] = jnp.broadcast_to(mean, mean_ref.shape)
     for part in (1, 0):
         for q in range(2):
             place = cross_ref.at[q, :, pl.ds(part * hw, hw)]
@@ -275,17 +316,19 @@
     )
     bf = jnp.bfloat16
     dma = pltpu.SemaphoreType.DMA
-    top_cov, cross_half, node_var = pl.pallas_call(
+    top_cov, cross_half, node_var, means = pl.pallas_call(
         fused,
         out_shape=(
             jax.ShapeDtypeStruct((tb, tb), jnp.float32),
             jax.ShapeDtypeStruct((2, tb, width), bf),
             jax.ShapeDtypeStruct((2, width), jnp.float32),
-        ),
-        in_specs=[pl.BlockSpec(memory_space=pl.ANY)] * 4,
+            jax.ShapeDtypeStruct((G, 128), jnp.float32),
+        ),
+        in_specs=[pl.BlockSpec(memory_space=pl.ANY)] * 4 + [pl.BlockSpec(memory_space=pltpu.VMEM)],
         out_specs=(
             pl.BlockSpec(memory_space=pltpu.VMEM),
             pl.BlockSpec(memory_space=pl.ANY),
+            pl.BlockSpec(memory_space=pltpu.VMEM),
             pl.BlockSpec(memory_space=pltpu.VMEM),
         ),
         scratch_shapes=[
@@ -299,21 +342,16 @@
             pltpu.VMEM((2, 8, hw), jnp.float32),
             pltpu.VMEM((8, 8, hw), jnp.float32),
             pltpu.VMEM((row_struct.shape[1], 8, hw), jnp.float32),
-            dma((20,)), dma((16,)), dma((4,)), dma((4,)), dma((4,)), dma((8,)), dma((8,)),
+            pltpu.VMEM((4, 2, G, 128), jnp.float32),
+            dma((24,)), dma((16,)), dma((4,)), dma((4,)), dma((4,)), dma((8,)), dma((8,)),
             dma((2,)), dma((2,)), dma((4,)), dma((4,)), dma((8,)), dma((8,)),
-            dma((1,)), dma((1,)),
+            dma((1,)), dma((1,)), dma((3,)), dma((4,)),
         ],
         compiler_params=pltpu.CompilerParams(
             collective_id=0, has_side_effects=True, vmem_limit_bytes=48 * 1024 * 1024
         ),
-    )(top_factor, off_block, kid_factor, keep)
-    cross_cov = cross_half.astype(jnp.float32)
-    onehot = (labels[:, :, None] == jnp.arange(G, dtype=jnp.int32)[None, None, :]).astype(
-        jnp.float32
-    )
-    local_counts = jnp.sum(onehot, axis=(0, 1))
-    label_sum, counts = lax.psum((jnp.einsum("kw,kwg->g", node_var, onehot), local_counts), "scol")
-    return (top_cov, cross_cov, node_var, label_sum / counts)
+    )(top_factor, off_block, kid_factor, keep, labels)
+    return (top_cov, cross_half.astype(jnp.float32), node_var, means[:, 0])
 
 
 def solution(mesh):

time: 154 us -> 151 us (0.981)
  blocking collectives: 22.5 us -> 0 us
  Pallas kernels: 124 us -> 142 us
    psum x1 -> x0, blocking collectives: 22.5 us -> none  [per_device_fused(): lax.psum((jnp.einsum('kw,kwg->g', node_var, onehot), local_counts), 'scol')]
    pallas_call x1, Pallas kernels: 124 us -> 142 us  [per_device_fused(): pl.pallas_call(fused, out_shape=(jax.ShapeDtypeStruct((tb, tb), jnp.float...]
where the time goes in v3:
time: 151 us
  Pallas kernels  142 us (94%)
  other arithmetic  5.06 us (3%)
  local copies, waits for them, and re-layouts  2.35 us (2%)
    pallas_call x1, Pallas kernels, per_device_fused(): pl.pallas_call(fused, out_shape=(jax.ShapeDtypeStruct((tb, tb), jnp.float...  142 us

profile of v3, /device:TPU:0, one launch (start us, length us, event | category | flops | bytes accessed | tf_op | source)
XLA Modules:
  0.0 150.5 jit_solution(10541344851471467796)
XLA Ops:
  0.6 0.0 copy-start.1
  0.7 0.8 compare_convert_fusion.1
  1.4 1.3 compare_select_fusion.f_ref
  2.7 0.0 copy-start
  2.7 0.1 broadcast_in_dim.12.keep_ref
  2.8 0.3 fusion
  3.1 0.0 copy-done.1
  3.2 0.2 broadcast_select_fusion.kid_ref
  3.4 0.1 copy-done
  3.4 142.4 %shard_map.84 = (f32[512,512]{1,0:T(8,128)S(1)}, bf16[2,512,1024]{2,1,0:T(8,128)(2,1)S(1)}, f32[2,1024]{1,0:T(2,128)S(1)}, f32[32,128]{1,0:T(8,128)S(1)}) custom-call(bf16[512,512]{1,0:T(8,128)(2,1)S(1)} %compare_select_fusion.f_ref, bf16[2,512,1024]{2,1,0:T(8,128)(2,1)} %off_ref.1, bf16[2,256,1024]{2,1,0:T(8,128)(2,1)S(1)} %broadcast_select_fusion.kid_ref, ...), custom_call_target="tpu_custom_call" | custom-call | tf_op jit(solution)/shard_map/pallas_call | solution.py:319
  145.8 0.6 slice_reduce_fusion
  146.5 2.5 %convert_element_type.15 = f32[2,512,1024]{2,1,0:T(8,128)} convert(bf16[2,512,1024]{2,1,0:T(8,128)(2,1)S(1)} %get-tuple-element.9) | non-fusion elementwise | flops 1048576 | bytes 6291456 | tf_op jit(solution)/shard_map/convert_element_type | solution.py:354
  149.0 1.0 copy.11
  149.9 0.6 copy.12
  (2 shorter events, 0.0 us)
Async XLA Ops:
  0.6 2.5 %copy-start.1 = (bf16[2,256,1024]{2,1,0:T(8,128)(2,1)S(1)}, bf16[2,256,1024]{2,1,0:T(8,128)(2,1)}, u32[]{:S(2)}) copy-start(bf16[2,256,1024]{2,1,0:T(8,128)(2,1)} %param.7) | copy-start | bytes 3145732
  2.7 0.7 copy-start

commit v4 on v3

--- a/solution.py
+++ b/solution.py
@@ -171,13 +171,14 @@
              jnp.maximum(z - 1, 0), d)
 
     for s in range(1, 4):
+        if s == 3:
+            start_inputs(0)
         pass_on(s - 1)
         r = order[s]
         c, _ = columns(r)
         arrived(r <= c, fall.at[r, c], f_recv.at[r * 4 + c])
         fan(s, r, fall.at[r, c])
     pass_on(3)
-    start_inputs(0)
     arrived(z >= 0, kept, k_recv.at[0])
     def outer_block(r, c):
         acc[...] = jnp.zeros_like(acc)
@@ -221,6 +222,12 @@
 
     def make_cross(part):
         cols = pl.ds(part * hw, hw)
+        def ship(i):
+            there = 2 * h + i
+            send(there != z, cbuf.at[part, i], cross_ref.at[slot, :, cols], c_send.at[part * 2 + i],
+                 c_recv.at[part * 2 + slot], there, home)
+            local(there == z, cbuf.at[part, i], cross_ref.at[slot, :, cols], c_recv.at[part * 2 + slot])
+
         theirs = prod.at[part, pl.ds(pl.multiple_of((1 - h) * 2 * tb, 2 * tb), 2 * tb), :]
         arrived(z >= 0, theirs, p_recv.at[part])
         for i in range(2):
@@ -232,16 +239,17 @@
                 own = prod[part, pl.ds(pl.multiple_of(half + i * tb + m * (tb // 2), tb // 2), tb // 2), :]
                 vsum[part] += jnp.sum((own.astype(jnp.float32) * total).reshape(tb // 16, 8, hw), axis=0)
                 cbuf[part, i, rows, :] = (-total).astype(jnp.bfloat16)
-            there = 2 * h + i
-            send(there != z, cbuf.at[part, i], cross_ref.at[slot, :, cols], c_send.at[part * 2 + i],
-                 c_recv.at[part * 2 + slot], there, home)
-            local(there == z, cbuf.at[part, i], cross_ref.at[slot, :, cols], c_recv.at[part * 2 + slot])
+            if part:
+                ship(i)
         for there in range(4):
             to_self = (there == z) & is_keeper
             place = part * 4 + slot * 2 + h
             send(jnp.logical_not(to_self), vsum.at[part], vgot.at[place], v_send.at[part * 4 + there],
                  v_recv.at[place], there, home)
             local(to_self, vsum.at[part], vgot.at[place], v_recv.at[place])
+        if not part:
+            ship(0)
+            ship(1)
 
     make_product(1)
     arrived(z <= d, fall.at[z, d], f_recv.at[z * 4 + d])

time: 151 us -> 152 us (level)
  the two profiles are of different devices: /device:TPU:0 before, /device:TPU:26 now
where the time goes in v4:
time: 152 us
  Pallas kernels  144 us (95%)
  other arithmetic  5.06 us (3%)
  local copies, waits for them, and re-layouts  2.35 us (2%)
    pallas_call x1, Pallas kernels, per_device_fused(): pl.pallas_call(fused, out_shape=(jax.ShapeDtypeStruct((tb, tb), jnp.float...  144 us

profile of v4, /device:TPU:26, one launch (start us, length us, event | category | flops | bytes accessed | tf_op | source)
XLA Modules:
  0.0 152.2 jit_solution(17189027896952159655)
XLA Ops:
  0.6 0.0 copy-start.1
  0.7 0.8 compare_convert_fusion.1
  1.4 1.3 compare_select_fusion.f_ref
  2.7 0.0 copy-start
  2.7 0.1 broadcast_in_dim.12.keep_ref
  2.8 0.3 fusion
  3.1 0.0 copy-done.1
  3.2 0.2 broadcast_select_fusion.kid_ref
  3.4 0.1 copy-done
  3.4 144.0 %shard_map.84 = (f32[512,512]{1,0:T(8,128)S(1)}, bf16[2,512,1024]{2,1,0:T(8,128)(2,1)S(1)}, f32[2,1024]{1,0:T(2,128)S(1)}, f32[32,128]{1,0:T(8,128)S(1)}) custom-call(bf16[512,512]{1,0:T(8,128)(2,1)S(1)} %compare_select_fusion.f_ref, bf16[2,512,1024]{2,1,0:T(8,128)(2,1)} %off_ref.1, bf16[2,256,1024]{2,1,0:T(8,128)(2,1)S(1)} %broadcast_select_fusion.kid_ref, ...), custom_call_target="tpu_custom_call" | custom-call | tf_op jit(solution)/shard_map/pallas_call | solution.py:327
  147.5 0.6 slice_reduce_fusion
  148.1 2.5 %convert_element_type.15 = f32[2,512,1024]{2,1,0:T(8,128)} convert(bf16[2,512,1024]{2,1,0:T(8,128)(2,1)S(1)} %get-tuple-element.9) | non-fusion elementwise | flops 1048576 | bytes 6291456 | tf_op jit(solution)/shard_map/convert_element_type | solution.py:362
  150.6 1.0 copy.11
  151.6 0.6 copy.12
  (2 shorter events, 0.0 us)
Async XLA Ops:
  0.6 2.5 %copy-start.1 = (bf16[2,256,1024]{2,1,0:T(8,128)(2,1)S(1)}, bf16[2,256,1024]{2,1,0:T(8,128)(2,1)}, u32[]{:S(2)}) copy-start(bf16[2,256,1024]{2,1,0:T(8,128)(2,1)} %param.7) | copy-start | bytes 3145732
  2.7 0.7 copy-start
